TPU v7x, 32 devices: a whole 2x2x4 slice. The times are simulated.
32 devices in a mesh: groups: 2 (over x), tensor: 8 (over z, y), side: 2 (over core).
Axes of the slice: x: 2, y: 2, z: 4, core: 2. Of those that a mesh axis runs over, the one named last changes fastest.
Arguments:
- hidden_in: bfloat16 [96, 16384], P('groups', ('tensor', 'side')), parts along dimension 0, may hold values from -600 to 600
- norm_gain: float32 [16384], replicated, may hold values from 0.1 to 1.9
- w_query: bfloat16 [16384, 16384], P(None, ('tensor', 'side')), may hold values from -0.046875 to 0.046875
- key_projection: bfloat16 [16384, 1024], P(None, ('tensor', 'side')), may hold values from -0.046875 to 0.046875
- value_projection: bfloat16 [16384, 1024], P(None, ('tensor', 'side')), may hold values from -0.046875 to 0.046875
- w_out: bfloat16 [16384, 16384], P(None, ('tensor', 'side')), may hold values from -0.046875 to 0.046875
- paged_key_cache: bfloat16 [512, 64, 1024], P(('groups', 'tensor', 'side')), parts along dimension 0, may hold values from -4 to 4
- paged_value_cache: bfloat16 [512, 64, 1024], P(('groups', 'tensor', 'side')), parts along dimension 0, may hold values from -4 to 4
- key_scale: float32 [512, 8], P(('groups', 'tensor', 'side')), parts along dimension 0, may hold values from 0.5 to 200
- value_page_scale: float32 [512, 8], P(('groups', 'tensor', 'side')), parts along dimension 0, may hold values from 0.5 to 2
- row_owner: int32 [96, 1], P('groups'), parts along dimension 0, may hold values from 0 to 15; in each aligned block of 48 rows (0 to 47, 48 to 95, ...) at most 4 rows name the same one
- lengths: int32 [96], P('groups'), parts along dimension 0, may hold values from 1 to 256, 7680 in all
- page_table: int32 [32, 16], P(('groups', 'tensor', 'side')), parts along dimension 0, may hold values from 0 to 15, each once within a row
Outputs:
- attn_out: bfloat16 [96, 16384], P('groups', ('tensor', 'side')), parts along dimension 0
There are 2 independent parts, one for each index of `groups`. A program takes and returns all parts, laid end to end along the dimension named above; an argument that names none is the same for every part. Nothing has to cross between parts.
Inputs may be any that keep to these rules, and one draw needn't show every extreme that they name: `row_owner`: at most 4 rows name one owner; some owner is named by exactly 4 rows and every owner by at least one. `lengths`: some row has exactly 256 cached tokens. Each row of page_table holds every number from 0 to 15 once.
All inputs are finite; a program needn't handle non-finite values.
Results may differ from a plain program's by a relative error of at most 0.006.
The roundings to bfloat16 on the way count: a program that leaves them out, or rounds other values in their place, can miss the bound.
Values may be sent and summed in bfloat16 or wider, within the bound.
A program may use at most 192 MiB of HBM per device.

v0:
```python
import math

import jax
import jax.numpy as jnp
from jax import lax
from jax.sharding import PartitionSpec as P

QUERY_HEADS = 128
KEY_VALUE_HEADS = 8
HEAD_SIZE = 128
PAGE_TOKENS = 64
SLOT_PAGES = 4
OWNER_ROW_SLOTS = 4
MAX_ROW_TOKENS = 256


def rotation_angles(vectors, token_position):
    half_size = vectors.shape[-1] // 2
    exponent = jnp.arange(half_size, dtype=jnp.float32) * (-2.0 / vectors.shape[-1])
    frequency = jnp.power(jnp.float32(500000.0), exponent)
    angles = token_position * frequency
    cosine = jnp.cos(angles)
    sine_part = jnp.sin(angles)
    first = vectors[..., :half_size]
    second = vectors[..., half_size:]
    return jnp.concatenate(
        [first * cosine - second * sine_part, second * cosine + first * sine_part], axis=-1
    )


def per_device(
    hidden_in,
    norm_gain,
    w_query,
    key_projection,
    value_projection,
    w_out,
    paged_key_cache,
    paged_value_cache,
    key_scale,
    value_page_scale,
    row_owner,
    lengths,
    page_table,
):
    owners = lax.axis_size(("tensor", "side"))
    my_index = lax.axis_index(("tensor", "side"))
    row_count = hidden_in.shape[0]
    query_group_count = QUERY_HEADS // KEY_VALUE_HEADS
    inv_root = 1.0 / math.sqrt(HEAD_SIZE)
    whole_rows = lax.all_gather(hidden_in, ("tensor", "side"), axis=1, tiled=True)
    widened = whole_rows.astype(jnp.float32)
    mean_square = jnp.mean(widened * widened, axis=1, keepdims=True)
    normed = (widened * lax.rsqrt(mean_square + 1e-05) * norm_gain).astype(jnp.bfloat16)
    query = jnp.dot(normed, w_query, preferred_element_type=jnp.float32).astype(jnp.bfloat16)
    key_new = jnp.dot(normed, key_projection, preferred_element_type=jnp.float32).astype(
        jnp.bfloat16
    )
    value_new = jnp.dot(normed, value_projection, preferred_element_type=jnp.float32).astype(
        jnp.bfloat16
    )
    owner_ids = row_owner[:, 0]
    row_numbers = jnp.arange(row_count)
    same_owner = owner_ids[:, None] == owner_ids[None, :]
    earlier = row_numbers[None, :] < row_numbers[:, None]
    slot_index = jnp.sum(jnp.where(same_owner & earlier, 1, 0), axis=1).astype(jnp.int32)
    destination = owner_ids * OWNER_ROW_SLOTS + slot_index
    packed = jnp.concatenate([query, key_new, value_new], axis=1)
    feature_count = packed.shape[1]
    one_hot = (jnp.arange(owners * OWNER_ROW_SLOTS)[:, None] == destination[None, :]).astype(
        jnp.bfloat16
    )
    outgoing = jnp.dot(one_hot, packed, preferred_element_type=jnp.float32).astype(jnp.bfloat16)
    received_part = lax.all_to_all(
        outgoing.reshape(owners, OWNER_ROW_SLOTS, 1, feature_count),
        ("tensor", "side"),
        split_axis=0,
        concat_axis=2,
        tiled=True,
    )
    received_part = received_part.reshape(OWNER_ROW_SLOTS, owners, feature_count)
    query_columns = query.shape[1]
    key_columns = key_new.shape[1]
    query_all = received_part[:, :, :query_columns].reshape(
        OWNER_ROW_SLOTS, QUERY_HEADS * HEAD_SIZE
    )
    every_key = received_part[:, :, query_columns : query_columns + key_columns].reshape(
        OWNER_ROW_SLOTS, KEY_VALUE_HEADS * HEAD_SIZE
    )
    every_value = received_part[:, :, query_columns + key_columns :].reshape(
        OWNER_ROW_SLOTS, KEY_VALUE_HEADS * HEAD_SIZE
    )
    mine = owner_ids == my_index
    slot_match = (jnp.arange(OWNER_ROW_SLOTS)[:, None] == slot_index[None, :]) & mine[None, :]
    slot_length = jnp.sum(jnp.where(slot_match, lengths[None, :], 0), axis=1)
    page_numbers = page_table[0].reshape(OWNER_ROW_SLOTS, SLOT_PAGES)
    stored_keys = paged_key_cache[page_numbers].reshape(
        OWNER_ROW_SLOTS, MAX_ROW_TOKENS, KEY_VALUE_HEADS, HEAD_SIZE
    )
    stored_values = paged_value_cache[page_numbers].reshape(
        OWNER_ROW_SLOTS, MAX_ROW_TOKENS, KEY_VALUE_HEADS, HEAD_SIZE
    )
    key_factor = (
        jnp.transpose(jnp.repeat(key_scale[page_numbers], PAGE_TOKENS, axis=1), (0, 2, 1))
        * inv_root
    )
    value_factor = jnp.transpose(
        jnp.repeat(value_page_scale[page_numbers], PAGE_TOKENS, axis=1), (0, 2, 1)
    )
    token_position = slot_length.astype(jnp.float32)[:, None, None]
    turned_query = rotation_angles(
        query_all.astype(jnp.float32).reshape(OWNER_ROW_SLOTS, QUERY_HEADS, HEAD_SIZE),
        token_position,
    ).astype(jnp.bfloat16)
    turned_query = turned_query.reshape(
        OWNER_ROW_SLOTS, KEY_VALUE_HEADS, query_group_count, HEAD_SIZE
    )
    turned_key = rotation_angles(
        every_key.astype(jnp.float32).reshape(OWNER_ROW_SLOTS, KEY_VALUE_HEADS, HEAD_SIZE),
        token_position,
    ).astype(jnp.bfloat16)
    scores = (
        jnp.einsum("cgjd,ctgd->cgjt", turned_query, stored_keys, preferred_element_type=jnp.float32)
        * key_factor[:, :, None, :]
    )
    own_score = (
        jnp.einsum("cgjd,cgd->cgj", turned_query, turned_key, preferred_element_type=jnp.float32)
        * inv_root
    )
    live = (jnp.arange(MAX_ROW_TOKENS)[None, :] < slot_length[:, None])[:, None, None, :]
    masked = jnp.where(live, scores, -jnp.inf)
    highest = jnp.maximum(jnp.max(masked, axis=-1), own_score)
    exponents = jnp.where(live, jnp.exp(masked - highest[..., None]), 0.0)
    own_exp = jnp.exp(own_score - highest)
    denominator = jnp.sum(exponents, axis=-1) + own_exp
    weights = (exponents / denominator[..., None] * value_factor[:, :, None, :]).astype(
        jnp.bfloat16
    )
    local_weight_sum = (own_exp / denominator).astype(jnp.bfloat16)
    blended_output = jnp.einsum(
        "cgjt,ctgd->cgjd", weights, stored_values, preferred_element_type=jnp.float32
    )
    blended_output = (
        blended_output
        + local_weight_sum.astype(jnp.float32)[..., None]
        * every_value.astype(jnp.float32).reshape(OWNER_ROW_SLOTS, KEY_VALUE_HEADS, HEAD_SIZE)[
            :, :, None, :
        ]
    )
    slot_results = blended_output.reshape(OWNER_ROW_SLOTS, QUERY_HEADS * HEAD_SIZE).astype(
        jnp.bfloat16
    )
    projected = jnp.dot(
        lax.all_gather(slot_results, ("tensor", "side"), axis=0, tiled=True),
        w_out,
        preferred_element_type=jnp.float32,
    )
    return jnp.take(projected, destination, axis=0).astype(jnp.bfloat16)


def solution(mesh):
    return jax.shard_map(
        per_device,
        mesh=mesh,
        in_specs=(
            P("groups", ("tensor", "side")),
            P(),
            P(None, ("tensor", "side")),
            P(None, ("tensor", "side")),
            P(None, ("tensor", "side")),
            P(None, ("tensor", "side")),
            P(("groups", "tensor", "side"), None, None),
            P(("groups", "tensor", "side"), None, None),
            P(("groups", "tensor", "side"), None),
            P(("groups", "tensor", "side"), None),
            P("groups", None),
            P("groups"),
            P(("groups", "tensor", "side"), None),
        ),
        out_specs=P("groups", ("tensor", "side")),
        check_vma=False,
    )
```

profile of v0, /device:TPU:1, one launch (start us, length us, event | category | flops | bytes accessed | tf_op | source)
XLA Modules:
  0.0 164.8 jit_solution(11813720719551885457)
XLA Ops:
  6.5 0.0 copy-start
  6.5 0.0 all-gather.4.cloned.1.call-start
  6.5 0.7 all-gather.4.cloned.1.call-update
  7.3 0.5 broadcast.145
  7.8 1.3 reduce.3
  9.1 0.1 reshape_squeeze.3
  9.2 0.1 reshape.201
  9.3 0.8 copy.50
  10.0 0.6 gather_fusion.1
  10.6 0.9 select_reduce_fusion
  11.5 0.7 broadcast_compare_fusion
  12.2 0.8 select_reduce_fusion.1
  13.0 0.7 multiply_add_fusion
  13.6 0.1 iota_compare_fusion.3
  13.7 38.1 %all-gather.4.cloned.1.call-done = bf16[48,16384]{1,0:T(8,128)(2,1)} async-done(((bf16[48,1024]{1,0:T(8,128)(2,1)}), bf16[48,16384]{1,0:T(8,128)(2,1)}) %all-gather.4.cloned.1.call-update) | async-done | bytes 1572880 | tf_op jit(solution)/shard_map/all_gather | solution.py:51
  51.8 1.9 %fusion = f32[48]{0:T(128)S(1)} fusion(bf16[48,16384]{1,0:T(8,128)(2,1)} %all-gather.4.cloned.1.call-done), kind=kLoop, calls=%fused_computation.7 | loop fusion | flops 2359248 | bytes 1573056 | tf_op jit(solution)/shard_map/reduce_sum | solution.py:53
  53.7 0.0 copy-done.2
  53.8 0.0 copy-start.3
  53.8 0.0 copy-start.6
  53.8 13.9 %convolution_convert_fusion.1 = bf16[48,1024]{1,0:T(8,128)(2,1)S(1)} fusion(bf16[16384,1024]{1,0:T(8,128)(2,1)} %param.15, bf16[48,16384]{1,0:T(8,128)(2,1)S(1)} %copy-done.2, f32[16384]{0:T(1024)} %param.14, f32[48]{0:T(128)S(1)} %add_rsqrt_fusion), kind=kOutput, calls=%fused_computation.19 | convolution fusion | flops 1613807616 | bytes 35291328 | tf_op jit(solution)/shard_map/dot_general | solution.py:55
  67.7 0.0 copy-done.3
  67.7 0.0 copy-done.6
  67.7 0.0 copy-start.7
  67.7 0.8 convolution_convert_fusion.2
  68.5 0.8 copy-done.7
  69.3 0.8 convolution_convert_fusion.3
  70.0 0.1 concatenate.16
  70.1 0.2 convolution_convert_fusion
  70.3 0.7 reshape.191
  71.0 3.8 %all-to-all-start = ((bf16[16,4,1,1152]{3,1,2,0:T(4,128)(2,1)}), bf16[16,4,1,1152]{3,1,2,0:T(4,128)(2,1)S(1)}, u32[]{:S(2)}, u32[]{:S(2)}) async-start(bf16[16,4,1,1152]{3,1,2,0:T(4,128)(2,1)} %bitcast.3), calls=%async_computation | async-start | bytes 294912 | tf_op jit(solution)/shard_map/all_to_all | solution.py:74
  74.8 0.2 all-gather.6.cloned.1.call-start
  75.0 0.0 copy-done
  75.0 2.0 %gather_fusion = bf16[16,64,1024]{2,1,0:T(8,128)(2,1)} fusion(bf16[16,64,1024]{2,1,0:T(8,128)(2,1)S(1)} %copy-done, s32[1024]{0:T(1024)S(1)} %pad_clamp_fusion.1), kind=kCustom, calls=%fused_computation | custom fusion | bytes 4194368 | tf_op jit(solution)/shard_map/gather | solution.py:97
  77.1 2.2 %copy.57 = bf16[128,8,8,128]{3,2,1,0:T(8,128)(2,1)S(1)} copy(bf16[128,8,8,128]{3,1,2,0:T(8,128)(2,1)} %bitcast.52) | data formatting | bytes 4194304
  79.3 0.1 copy.51
  79.4 0.1 broadcast_in_dim.85
  79.5 0.1 mul.200
  79.6 3.6 %gather_fusion.3 = bf16[16,64,1024]{2,1,0:T(8,128)(2,1)} fusion(bf16[16,64,1024]{2,1,0:T(8,128)(2,1)} %param.20, s32[1024]{0:T(1024)S(1)} %pad_clamp_fusion.1), kind=kCustom, calls=%fused_computation.3 | custom fusion | bytes 4194368 | tf_op jit(solution)/shard_map/gather | solution.py:100
  83.2 3.6 %copy.58 = bf16[128,8,8,128]{3,2,1,0:T(8,128)(2,1)} copy(bf16[128,8,8,128]{3,1,2,0:T(8,128)(2,1)} %bitcast.53) | data formatting | bytes 4194304
  86.7 0.0 copy-done.4
  86.7 0.1 copy.52
  86.8 0.6 gather_fusion.2
  87.4 0.1 copy.53
  87.5 0.1 broadcast_in_dim.88
  87.6 0.1 reshape.194
  87.7 0.1 multiply_cosine_fusion
  87.8 0.0 all-to-all-done
  87.8 0.1 slice_convert_fusion.1
  87.9 0.1 reshape.197
  88.1 0.1 subtract_convert_fusion.1
  88.1 0.1 subtract_convert_fusion
  88.3 0.1 maximum_bitcast_fusion
  88.4 0.2 fusion.26
  88.6 0.8 fusion.38
  89.4 0.3 fusion.19
  89.7 0.1 reshape.198
  89.8 2.1 %fusion.16 = bf16[4,8,16,128]{3,2,1,0:T(8,128)(2,1)S(1)} fusion(bf16[4,256,8,128]{3,2,1,0:T(8,128)(2,1)} %bitcast.54, f32[4,8,16,256]{3,2,1,0:T(8,128)S(1)} %get-tuple-element.18, f32[4,8,256]{2,1,0:T(8,128)S(1)} %bitcast.64, f32[4,8,16]{2,1,0:T(8,128)S(1)} %get-tuple-element.12, f32[4,8,16]{2,1,0:T(8,128)S(1)} %multiply_maximum_fusion, ...), kind=kOutput, calls=%fused_computation.18 | convolution fusion | flops 34406400 | bytes 2808832 | tf_op jit(solution)/shard_map/cgjt,ctgd->cgjd/dot_general | solution.py:140
  91.9 0.7 reshape.247
  92.6 0.0 all-gather.6.cloned.1.call-update
  92.7 42.7 %all-gather.6.cloned.1.call-done = bf16[16,4,16384]{2,1,0:T(4,128)(2,1)} async-done(((bf16[1,4,16384]{2,1,0:T(4,128)(2,1)}), bf16[16,4,16384]{2,1,0:T(4,128)(2,1)}) %all-gather.6.cloned.1.call-update) | async-done | bytes 2097168 | tf_op jit(solution)/shard_map/all_gather | solution.py:154
  135.3 4.0 %reshape.248 = bf16[64,16384]{1,0:T(8,128)(2,1)} reshape(bf16[16,4,16384]{2,1,0:T(4,128)(2,1)} %all-gather.6.cloned.1.call-done) | data formatting | bytes 4194304
  139.3 17.2 %fusion.39 = bf16[64,1024]{1,0:T(8,128)(2,1)S(1)} fusion(bf16[64,16384]{1,0:T(8,128)(2,1)} %reshape.248, bf16[16384,1024]{1,0:T(8,128)(2,1)} %param.18), kind=kOutput, calls=%fused_computation.74 | convolution fusion | flops 2147483648 | bytes 35782656 | tf_op jit(solution)/shard_map/dot_general | solution.py:153
  156.5 0.7 gather_fusion.4
  157.2 0.7 select_convert_fusion
  (19 shorter events, 0.2 us)
Async XLA Ops:
  6.5 68.5 %copy-start = (bf16[16,64,1024]{2,1,0:T(8,128)(2,1)S(1)}, bf16[16,64,1024]{2,1,0:T(8,128)(2,1)}, u32[]{:S(2)}) copy-start(bf16[16,64,1024]{2,1,0:T(8,128)(2,1)} %param.19) | copy-start | bytes 6291460
  6.5 45.3 %all-gather.4.cloned.1.call-start = ((), (), s32[]{:S(2)}) async-start(), calls=%async_computation.1 | async-start | bytes 1671168 | tf_op jit(solution)/shard_map/all_gather | solution.py:51
  51.8 2.0 %copy-start.2 = (bf16[48,16384]{1,0:T(8,128)(2,1)S(1)}, bf16[48,16384]{1,0:T(8,128)(2,1)}, u32[]{:S(2)}) copy-start(bf16[48,16384]{1,0:T(8,128)(2,1)} %all-gather.4.cloned.1.call-done) | copy-start | bytes 4718596
  53.8 13.9 %copy-start.3 = (f32[16384]{0:T(1024)S(1)}, f32[16384]{0:T(1024)}, u32[]{:S(2)}) copy-start(f32[16384]{0:T(1024)} %param.14) | copy-start | bytes 196612
  53.8 13.9 %copy-start.6 = (bf16[16384,64]{0,1:T(8,128)(2,1)S(1)}, bf16[16384,64]{0,1:T(8,128)(2,1)}, u32[]{:S(2)}) copy-start(bf16[16384,64]{0,1:T(8,128)(2,1)} %param.17) | copy-start | bytes 6291460
  67.7 1.6 copy-start.7
  71.0 16.8 %all-to-all-start = ((bf16[16,4,1,1152]{3,1,2,0:T(4,128)(2,1)}), bf16[16,4,1,1152]{3,1,2,0:T(4,128)(2,1)S(1)}, u32[]{:S(2)}, u32[]{:S(2)}) async-start(bf16[16,4,1,1152]{3,1,2,0:T(4,128)(2,1)} %bitcast.3), calls=%async_computation | async-start | bytes 294912 | tf_op jit(solution)/shard_map/all_to_all | solution.py:74
  74.8 60.5 %all-gather.6.cloned.1.call-start = ((), (), s32[]{:S(2)}) async-start(), calls=%async_computation.2 | async-start | bytes 2228224 | tf_op jit(solution)/shard_map/all_gather | solution.py:154
  83.2 3.6 %copy-start.4 = (f32[16,8]{0,1:T(8,128)S(1)}, f32[16,8]{0,1:T(8,128)}, u32[]{:S(2)}) copy-start(f32[16,8]{0,1:T(8,128)} %param.22) | copy-start | bytes 1540
  89.8 2.8 %copy-start.5 = (s32[48,1]{0,1:T(1,128)S(1)}, s32[48,1]{0,1:T(1,128)}, u32[]{:S(2)}) copy-start(s32[48,1]{0,1:T(1,128)} %param.23) | copy-start | bytes 580
  139.3 18.7 %copy-start.1 = (bf16[16,64,1024]{2,1,0:T(8,128)(2,1)S(1)}, bf16[16,64,1024]{2,1,0:T(8,128)(2,1)}, u32[]{:S(2)}) copy-start(bf16[16,64,1024]{2,1,0:T(8,128)(2,1)} %param.19) | copy-start | bytes 6291460
Sparse Core Ops, SparseCore 0:
  9.5 42.2 all-gather.3
  92.7 42.5 all-gather.5
where the time goes:
time: 165 us
  waiting for transfers between devices  81.5 us (49%)
  matrix products  35.9 us (22%)
  local copies, waits for them, and re-layouts  21.8 us (13%)
  between operations  13.6 us (8%)
  other arithmetic  7.92 us (5%)
  starting transfers between devices  3.98 us (2%)
    all_gather x1, waiting for transfers between devices, per_device(): lax.all_gather(slot_results, ('tensor', 'side'), axis=0, tiled=True)  42.7 us
    all_gather x1, waiting for transfers between devices, per_device(): lax.all_gather(hidden_in, ('tensor', 'side'), axis=1, tiled=True)  38.1 us
    dot_general x1, matrix products, per_device(): jnp.dot(lax.all_gather(slot_results, ('tensor', 'side'), axis=0, tiled=Tr...  17.2 us
    dot_general x1, matrix products, per_device(): jnp.dot(normed, w_query, preferred_element_type=jnp.float32)  13.9 us
    unnamed x23, local copies, waits for them, and re-layouts  12.7 us
    all_to_all x1, starting transfers between devices, per_device(): lax.all_to_all(outgoing.reshape(owners, OWNER_ROW_SLOTS, 1, feature_count...  3.76 us
    gather x1, local copies, waits for them, and re-layouts, per_device(): paged_value_cache[page_numbers]  3.57 us
  transfers between devices with their start and end apart: 3, of which 2 were waited for; matrix products, arithmetic and copies ran while one was open for 12% of the time, Pallas kernels for 0%

commit v1 on v0

v1 whole, which is shorter than its diff:
```python
import functools
import math

import jax
import jax.numpy as jnp
from jax import lax
from jax.experimental import pallas as pl
from jax.experimental.pallas import tpu as pltpu
from jax.sharding import PartitionSpec as P

QUERY_HEADS = 128
KEY_VALUE_HEADS = 8
HEAD_SIZE = 128
PAGE_TOKENS = 64
SLOT_PAGES = 4
OWNER_ROW_SLOTS = 4
MAX_ROW_TOKENS = 256


def rotation_angles(vectors, token_position):
    half_size = vectors.shape[-1] // 2
    exponent = jnp.arange(half_size, dtype=jnp.float32) * (-2.0 / vectors.shape[-1])
    frequency = jnp.power(jnp.float32(500000.0), exponent)
    angles = token_position * frequency
    cosine = jnp.cos(angles)
    sine_part = jnp.sin(angles)
    first = vectors[..., :half_size]
    second = vectors[..., half_size:]
    return jnp.concatenate(
        [first * cosine - second * sine_part, second * cosine + first * sine_part], axis=-1
    )

MESH = pl.DeviceIdType.MESH
GROUP_QUERIES = QUERY_HEADS // KEY_VALUE_HEADS
GROUP_WIDTH = GROUP_QUERIES * HEAD_SIZE
INV_ROOT = 1.0 / math.sqrt(HEAD_SIZE)


def place():
    tensor = lax.axis_index("tensor")
    return tensor // 2, lax.rem(tensor, 2), lax.axis_index("side"), lax.axis_size("tensor") // 2


def line_order(z, count):
    sign = 1 - 2 * (z // (count // 2))
    return [lax.rem(z + sign * k + count, count) for k in range(count)]


def enter():
    z, y, s, count = place()
    barrier = pltpu.get_barrier_semaphore()
    peers = [(zz * 2 + y, s) for zz in line_order(z, count)[1:]]
    peers += [(z * 2 + 1 - y, s), (z * 2 + y, 1 - s)]
    for tensor, side in peers:
        pl.semaphore_signal(
            barrier, inc=1, device_id={"tensor": tensor, "side": side}, device_id_type=MESH
        )
    pl.semaphore_wait(barrier, len(peers))


def gather(buffer, send_sems, recv_sems):
    z, y, s, count = place()
    line = line_order(z, count)
    started = []

    def index(zz, yy, ss):
        return (zz * 2 + yy) * 2 + ss

    def send(block, tensor, side):
        copy = pltpu.make_async_remote_copy(
            src_ref=buffer.at[block],
            dst_ref=buffer.at[block],
            send_sem=send_sems.at[len(started)],
            recv_sem=recv_sems.at[block],
            device_id={"tensor": tensor, "side": side},
            device_id_type=MESH,
        )
        copy.start()
        started.append(copy)

    def arrived(block):
        pltpu.make_async_remote_copy(
            src_ref=buffer.at[block],
            dst_ref=buffer.at[block],
            send_sem=send_sems.at[0],
            recv_sem=recv_sems.at[block],
            device_id={"tensor": z * 2 + y, "side": 1 - s},
            device_id_type=MESH,
        ).wait_recv()

    me = index(z, y, s)
    for zz in line[1:]:
        send(me, zz * 2 + y, s)
    send(me, z * 2 + 1 - y, s)
    send(me, z * 2 + y, 1 - s)
    for k in range(1, count + 1):
        if k < count:
            block = index(line[k], y, s)
            arrived(block)
            send(block, z * 2 + 1 - y, s)
            send(block, z * 2 + y, 1 - s)
        block = index(line[k - 1], 1 - y, s)
        arrived(block)
        send(block, z * 2 + y, 1 - s)
    for zz in line:
        for yy in (y, 1 - y):
            arrived(index(zz, yy, 1 - s))
    return started


def project_kernel(
    owners, x_ref, gain_ref, wq_hbm, key_hbm, value_hbm, out_ref,
    buffer, wq_ref, kv_ref, total, total_kv, w_sems, kv_sems, send_sems, recv_sems,
):
    depth = x_ref.shape[1]
    kv_columns = key_hbm.shape[0]
    query_columns = wq_hbm.shape[1]

    def weights(c):
        rows = pl.ds(pl.multiple_of(c * depth, depth), depth)
        return pltpu.make_async_copy(wq_hbm.at[rows, :], wq_ref.at[rows, :], w_sems.at[c])

    key_copy = pltpu.make_async_copy(key_hbm, kv_ref.at[0], kv_sems.at[0])
    value_copy = pltpu.make_async_copy(value_hbm, kv_ref.at[1], kv_sems.at[1])
    key_copy.start()
    value_copy.start()

    @pl.loop(0, owners)
    def _(c):
        weights(c).start()

    z, y, s, _ = place()
    buffer[(z * 2 + y) * 2 + s] = x_ref[...]
    enter()
    started = gather(buffer, send_sems, recv_sems)

    def squares(c, acc):
        x = buffer[c].astype(jnp.float32)
        return acc + jnp.sum(x * x, axis=1, keepdims=True)

    sums = lax.fori_loop(0, owners, squares, jnp.zeros((x_ref.shape[0], 1), jnp.float32))
    scale = lax.rsqrt(sums * (1.0 / (owners * depth)) + 1e-05)
    total[...] = jnp.zeros_like(total)
    total_kv[...] = jnp.zeros_like(total_kv)
    key_copy.wait()
    value_copy.wait()

    @pl.loop(0, owners)
    def _(c):
        columns = pl.ds(pl.multiple_of(c * depth, depth), depth)
        x = buffer[c].astype(jnp.float32)
        normed = (x * scale * gain_ref[pl.ds(c, 1), :]).astype(jnp.bfloat16)
        both = kv_ref[:, :, columns]
        if kv_columns % 16 == 0:
            both = both.reshape(2 * kv_columns, depth)
            total_kv[...] += lax.dot_general(
                normed, both, (((1,), (1,)), ((), ())), preferred_element_type=jnp.float32
            )
        else:
            for half in range(2):
                total_kv[:, half * kv_columns : (half + 1) * kv_columns] += lax.dot_general(
                    normed, both[half], (((1,), (1,)), ((), ())),
                    preferred_element_type=jnp.float32,
                )
        weights(c).wait()
        total[...] += jnp.dot(normed, wq_ref[columns, :], preferred_element_type=jnp.float32)

    out_ref[:, :query_columns] = total[...].astype(jnp.bfloat16)
    out_ref[:, query_columns:] = total_kv[...].astype(jnp.bfloat16)
    for copy in started:
        copy.wait_send()


def project(owners, hidden_in, norm_gain, w_query, key_projection, value_projection):
    rows, depth = hidden_in.shape
    columns, kv_columns = w_query.shape[1], key_projection.shape[1]
    sends = owners - 1
    vmem, anywhere = pl.BlockSpec(memory_space=pltpu.VMEM), pl.BlockSpec(memory_space=pl.ANY)
    return pl.pallas_call(
        functools.partial(project_kernel, owners),
        out_shape=jax.ShapeDtypeStruct((rows, columns + 2 * kv_columns), jnp.bfloat16),
        in_specs=[vmem, vmem, anywhere, anywhere, anywhere],
        out_specs=vmem,
        scratch_shapes=[
            pltpu.VMEM((owners, rows, depth), jnp.bfloat16),
            pltpu.VMEM(w_query.shape, jnp.bfloat16),
            pltpu.VMEM((2, kv_columns, owners * depth), jnp.bfloat16),
            pltpu.VMEM((rows, columns), jnp.float32),
            pltpu.VMEM((rows, 2 * kv_columns), jnp.float32),
            pltpu.SemaphoreType.DMA((owners,)),
            pltpu.SemaphoreType.DMA((2,)),
            pltpu.SemaphoreType.DMA((sends,)),
            pltpu.SemaphoreType.DMA((owners,)),
        ],
        compiler_params=pltpu.CompilerParams(
            collective_id=0, has_side_effects=True, vmem_limit_bytes=46 * 2**20
        ),
    )(hidden_in, norm_gain.reshape(owners, depth), w_query, key_projection.T, value_projection.T)


def attend_kernel(
    owners, wo_hbm, keys_ref, values_ref, query_ref, key_ref, value_ref, key_factor_ref,
    value_factor_ref, live_ref, destination_ref, out_ref,
    wo_ref, mixed, buffer, picked, total, w_sems, send_sems, recv_sems,
):
    rows = out_ref.shape[0]
    tokens = keys_ref.shape[0]
    slot_queries = OWNER_ROW_SLOTS * GROUP_QUERIES

    def weights(g):
        part = pl.ds(pl.multiple_of(g * GROUP_WIDTH, GROUP_WIDTH), GROUP_WIDTH)
        return pltpu.make_async_copy(wo_hbm.at[part, :], wo_ref.at[part, :], w_sems.at[g])

    @pl.loop(0, KEY_VALUE_HEADS)
    def _(g):
        weights(g).start()

    def spread(block):
        wide = jnp.broadcast_to(
            block[:, None, :], (OWNER_ROW_SLOTS, GROUP_QUERIES, block.shape[-1])
        )
        return wide.reshape(slot_queries, block.shape[-1])

    live = spread(live_ref[...]) > 0.5
    for g in range(KEY_VALUE_HEADS):
        columns = slice(g * HEAD_SIZE, (g + 1) * HEAD_SIZE)
        query = query_ref[g]
        scores = lax.dot_general(
            query, keys_ref[:, columns], (((1,), (1,)), ((), ())),
            preferred_element_type=jnp.float32,
        ) * key_factor_ref[g : g + 1, :]
        own = jnp.sum(
            query.astype(jnp.float32) * spread(key_ref[:, columns]), axis=1, keepdims=True
        ) * INV_ROOT
        masked = jnp.where(live, scores, -jnp.inf)
        highest = jnp.maximum(jnp.max(masked, axis=1, keepdims=True), own)
        exponents = jnp.exp(masked - highest)
        own_exp = jnp.exp(own - highest)
        inverse = 1.0 / (jnp.sum(exponents, axis=1, keepdims=True) + own_exp)
        probability = (exponents * inverse * value_factor_ref[g : g + 1, :]).astype(jnp.bfloat16)
        own_weight = (own_exp * inverse).astype(jnp.bfloat16).astype(jnp.float32)
        mixed[g * slot_queries : (g + 1) * slot_queries, :] = jnp.dot(
            probability, values_ref[:, columns], preferred_element_type=jnp.float32
        ) + own_weight * spread(value_ref[:, columns])

    z, y, s, _ = place()
    me = (z * 2 + y) * 2 + s
    block_rows = KEY_VALUE_HEADS * OWNER_ROW_SLOTS
    for j in range(GROUP_QUERIES):
        buffer[me, :, j * HEAD_SIZE : (j + 1) * HEAD_SIZE] = mixed[
            pl.ds(j, block_rows, stride=GROUP_QUERIES), :
        ].astype(jnp.bfloat16)
    enter()
    started = gather(buffer, send_sems, recv_sems)

    per = min(owners, 16)
    step = KEY_VALUE_HEADS if owners <= 16 else 1
    lane = lax.broadcasted_iota(jnp.int32, (rows, per * block_rows), 1)
    slot = (lane >> 5) * OWNER_ROW_SLOTS + (lane & 3)
    head = (lane >> 2) & 7

    def pick_block(block):
        everything = buffer[pl.ds(block * per, per)].reshape(per * block_rows, GROUP_WIDTH)
        wanted = destination_ref[...] - block * (per * OWNER_ROW_SLOTS)
        chosen = jnp.where(slot == wanted, head, -1)
        for first in range(0, KEY_VALUE_HEADS, step):
            pick = jnp.concatenate(
                [
                    jnp.where(chosen == first + g, 1.0, 0.0).astype(jnp.bfloat16)
                    for g in range(step)
                ],
                axis=0,
            )
            found = (
                jnp.dot(pick, everything, preferred_element_type=jnp.float32)
                .astype(jnp.bfloat16)
                .reshape(step, rows, GROUP_WIDTH)
            )
            if per == owners:
                picked[first : first + step] = found
            else:
                picked[first : first + step] += found

    if per == owners:
        pick_block(0)
    else:
        picked[...] = jnp.zeros_like(picked)
        pl.loop(0, owners // per)(pick_block)
    total[...] = jnp.zeros_like(total)

    @pl.loop(0, KEY_VALUE_HEADS)
    def _(g):
        weights(g).wait()
        part = pl.ds(pl.multiple_of(g * GROUP_WIDTH, GROUP_WIDTH), GROUP_WIDTH)
        total[...] += jnp.dot(picked[g], wo_ref[part, :], preferred_element_type=jnp.float32)

    out_ref[...] = total[...].astype(jnp.bfloat16)
    for copy in started:
        copy.wait_send()


def attend(owners, rows, w_out, *operands):
    sends = owners - 1
    block_rows = KEY_VALUE_HEADS * OWNER_ROW_SLOTS
    vmem, anywhere = pl.BlockSpec(memory_space=pltpu.VMEM), pl.BlockSpec(memory_space=pl.ANY)
    return pl.pallas_call(
        functools.partial(attend_kernel, owners),
        out_shape=jax.ShapeDtypeStruct((rows, w_out.shape[1]), jnp.bfloat16),
        in_specs=[anywhere] + [vmem] * len(operands),
        out_specs=vmem,
        scratch_shapes=[
            pltpu.VMEM(w_out.shape, jnp.bfloat16),
            pltpu.VMEM((block_rows * GROUP_QUERIES, HEAD_SIZE), jnp.float32),
            pltpu.VMEM((owners, block_rows, GROUP_WIDTH), jnp.bfloat16),
            pltpu.VMEM((KEY_VALUE_HEADS, rows, GROUP_WIDTH), jnp.bfloat16),
            pltpu.VMEM((rows, w_out.shape[1]), jnp.float32),
            pltpu.SemaphoreType.DMA((KEY_VALUE_HEADS,)),
            pltpu.SemaphoreType.DMA((sends,)),
            pltpu.SemaphoreType.DMA((owners,)),
        ],
        compiler_params=pltpu.CompilerParams(
            collective_id=1, has_side_effects=True, vmem_limit_bytes=56 * 2**20
        ),
    )(w_out, *operands)


def per_device(
    hidden_in,
    norm_gain,
    w_query,
    key_projection,
    value_projection,
    w_out,
    paged_key_cache,
    paged_value_cache,
    key_scale,
    value_page_scale,
    row_owner,
    lengths,
    page_table,
):
    owners = lax.axis_size(("tensor", "side"))
    my_index = lax.axis_index(("tensor", "side"))
    row_count = hidden_in.shape[0]
    query_group_count = QUERY_HEADS // KEY_VALUE_HEADS
    packed = project(owners, hidden_in, norm_gain, w_query, key_projection, value_projection)
    owner_ids = row_owner[:, 0]
    row_numbers = jnp.arange(row_count)
    same_owner = owner_ids[:, None] == owner_ids[None, :]
    earlier = row_numbers[None, :] < row_numbers[:, None]
    slot_index = jnp.sum(jnp.where(same_owner & earlier, 1, 0), axis=1).astype(jnp.int32)
    destination = owner_ids * OWNER_ROW_SLOTS + slot_index
    feature_count = packed.shape[1]
    one_hot = (jnp.arange(owners * OWNER_ROW_SLOTS)[:, None] == destination[None, :]).astype(
        jnp.bfloat16
    )
    outgoing = jnp.dot(one_hot, packed, preferred_element_type=jnp.float32).astype(jnp.bfloat16)
    received_part = lax.all_to_all(
        outgoing.reshape(owners, OWNER_ROW_SLOTS, 1, feature_count),
        ("tensor", "side"),
        split_axis=0,
        concat_axis=2,
        tiled=True,
    )
    received_part = received_part.reshape(OWNER_ROW_SLOTS, owners, feature_count)
    query_columns = w_query.shape[1]
    key_columns = key_projection.shape[1]
    query_all = received_part[:, :, :query_columns].reshape(
        OWNER_ROW_SLOTS, QUERY_HEADS * HEAD_SIZE
    )
    every_key = received_part[:, :, query_columns : query_columns + key_columns].reshape(
        OWNER_ROW_SLOTS, KEY_VALUE_HEADS * HEAD_SIZE
    )
    every_value = received_part[:, :, query_columns + key_columns :].reshape(
        OWNER_ROW_SLOTS, KEY_VALUE_HEADS * HEAD_SIZE
    )
    mine = owner_ids == my_index
    slot_match = (jnp.arange(OWNER_ROW_SLOTS)[:, None] == slot_index[None, :]) & mine[None, :]
    slot_length = jnp.sum(jnp.where(slot_match, lengths[None, :], 0), axis=1)
    pages = page_table.shape[1]
    page_slot = jnp.arange(pages)
    holds = page_table[0][:, None] == jnp.arange(pages)[None, :]
    page_place = jnp.sum(jnp.where(holds, page_slot[:, None], 0), axis=0)
    token_in_row = (
        (page_place % SLOT_PAGES)[:, None] * PAGE_TOKENS + jnp.arange(PAGE_TOKENS)[None, :]
    ).reshape(1, pages * PAGE_TOKENS)
    token_slot = jnp.repeat(page_place // SLOT_PAGES, PAGE_TOKENS)[None, :]
    live = (
        (token_slot == jnp.arange(OWNER_ROW_SLOTS)[:, None])
        & (token_in_row < slot_length[:, None])
    ).astype(jnp.float32)
    key_factor = jnp.repeat(key_scale.T, PAGE_TOKENS, axis=1) * INV_ROOT
    value_factor = jnp.repeat(value_page_scale.T, PAGE_TOKENS, axis=1)
    token_position = slot_length.astype(jnp.float32)[:, None, None]
    turned_query = rotation_angles(
        query_all.astype(jnp.float32).reshape(OWNER_ROW_SLOTS, QUERY_HEADS, HEAD_SIZE),
        token_position,
    ).astype(jnp.bfloat16)
    turned_query = jnp.transpose(
        turned_query.reshape(
            OWNER_ROW_SLOTS, KEY_VALUE_HEADS, query_group_count, HEAD_SIZE
        ),
        (1, 0, 2, 3),
    ).reshape(KEY_VALUE_HEADS, OWNER_ROW_SLOTS * query_group_count, HEAD_SIZE)
    turned_key = (
        rotation_angles(
            every_key.astype(jnp.float32).reshape(OWNER_ROW_SLOTS, KEY_VALUE_HEADS, HEAD_SIZE),
            token_position,
        )
        .astype(jnp.bfloat16)
        .astype(jnp.float32)
        .reshape(OWNER_ROW_SLOTS, KEY_VALUE_HEADS * HEAD_SIZE)
    )
    return attend(
        owners,
        row_count,
        w_out,
        paged_key_cache.reshape(pages * PAGE_TOKENS, KEY_VALUE_HEADS * HEAD_SIZE),
        paged_value_cache.reshape(pages * PAGE_TOKENS, KEY_VALUE_HEADS * HEAD_SIZE),
        turned_query,
        turned_key,
        every_value.astype(jnp.float32),
        key_factor,
        value_factor,
        live,
        destination.astype(jnp.int32)[:, None],
    )


def solution(mesh):
    return jax.shard_map(
        per_device,
        mesh=mesh,
        in_specs=(
            P("groups", ("tensor", "side")),
            P(),
            P(None, ("tensor", "side")),
            P(None, ("tensor", "side")),
            P(None, ("tensor", "side")),
            P(None, ("tensor", "side")),
            P(("groups", "tensor", "side"), None, None),
            P(("groups", "tensor", "side"), None, None),
            P(("groups", "tensor", "side"), None),
            P(("groups", "tensor", "side"), None),
            P("groups", None),
            P("groups"),
            P(("groups", "tensor", "side"), None),
        ),
        out_specs=P("groups", ("tensor", "side")),
        check_vma=False,
    )
```

time: 165 us -> 95.4 us (0.58)
  waiting for transfers between devices: 81.5 us -> 3.53 us
  Pallas kernels: 0 us -> 71.5 us
  matrix products: 35.9 us -> 0.17 us
  between operations: 13.6 us -> 0.13 us
  local copies, waits for them, and re-layouts: 21.8 us -> 11.7 us
  other arithmetic: 7.92 us -> 3.19 us
    all_gather x2 -> x0, waiting for transfers between devices: 80.8 us -> none  [the longest x1 42.7 us: per_device(): lax.all_gather(slot_results, ('tensor', 'side'), axis=0, tiled=True)]
    pallas_call x0 -> x2, Pallas kernels: none -> 71.5 us  [the longest x1 37.5 us: attend(): pl.pallas_call(functools.partial(attend_kernel, owners), out_shape=jax.Sh...]
    dot_general x7 -> x0, matrix products: 35.8 us -> none  [the longest x1 17.2 us: per_device(): jnp.dot(lax.all_gather(slot_results, ('tensor', 'side'), axis=0, tiled=Tr...]
    gather x6 -> x0, local copies, waits for them, and re-layouts: 7.49 us -> none  [the longest x1 3.57 us: per_device(): paged_value_cache[page_numbers]]
    unnamed x23 -> x18, local copies, waits for them, and re-layouts: 12.7 us -> 6.24 us
    all_to_all x1, waiting for transfers between devices: 0.01 us -> 3.53 us  [per_device(): lax.all_to_all(outgoing.reshape(owners, OWNER_ROW_SLOTS, 1, feature_count...]
    reduce_sum x2 -> x1, other arithmetic: 2.21 us -> 0.09 us  [per_device(): page_place = jnp.sum(jnp.where(holds, page_slot[:, None], 0), axis=0)]
  transfers between devices with their start and end apart: 3 -> 1, of which waited for: 2 -> 1; matrix products, arithmetic and copies ran while one was open for 12% -> 4% of each run, Pallas kernels for 0% -> 0%
where the time goes in v1:
time: 95.4 us; the launch traced here: 95 us
  Pallas kernels  71.5 us (75%)
  local copies, waits for them, and re-layouts  11.7 us (12%)
  starting transfers between devices  4.74 us (5%)
  waiting for transfers between devices  3.53 us (4%)
  other arithmetic  3.19 us (3%)
    pallas_call x1, Pallas kernels, attend(): pl.pallas_call(functools.partial(attend_kernel, owners), out_shape=jax.Sh...  37.5 us
    pallas_call x1, Pallas kernels, project(): pl.pallas_call(functools.partial(project_kernel, owners), out_shape=jax.S...  34 us
    unnamed x18, local copies, waits for them, and re-layouts  6.24 us
    all_to_all x1, starting transfers between devices, per_device(): lax.all_to_all(outgoing.reshape(owners, OWNER_ROW_SLOTS, 1, feature_count...  4.74 us
    all_to_all x1, waiting for transfers between devices, per_device(): lax.all_to_all(outgoing.reshape(owners, OWNER_ROW_SLOTS, 1, feature_count...  3.53 us
  transfers between devices with their start and end apart: 1, of which 1 were waited for; matrix products, arithmetic and copies ran while one was open for 4% of the time, Pallas kernels for 0%

profile of v1, /device:TPU:1, one launch (start us, length us, event | category | flops | bytes accessed | tf_op | source)
XLA Modules:
  0.0 95.0 jit_solution(10776059501147344350)
XLA Ops:
  0.0 0.9 select_reduce_fusion
  0.9 0.7 multiply_add_fusion
  1.6 0.9 reshape.166.gain_ref
  2.4 0.0 copy-start
  2.4 1.6 %copy-done = bf16[16384,64]{0,1:T(8,128)(2,1)S(1)} copy-done((bf16[16384,64]{0,1:T(8,128)(2,1)S(1)}, bf16[16384,64]{0,1:T(8,128)(2,1)}, u32[]{:S(2)}) %copy-start) | copy-done | bytes 2097176
  4.0 0.0 copy-start.1
  4.0 1.6 %copy-done.1 = bf16[16384,64]{0,1:T(8,128)(2,1)S(1)} copy-done((bf16[16384,64]{0,1:T(8,128)(2,1)S(1)}, bf16[16384,64]{0,1:T(8,128)(2,1)}, u32[]{:S(2)}) %copy-start.1) | copy-done | bytes 2097176
  5.6 0.0 copy-start.2
  5.6 0.9 copy-done.2
  6.5 0.0 copy-start.7
  6.5 0.0 copy-start.5
  6.5 0.0 copy-start.6
  6.5 0.0 copy-start.4
  6.5 0.0 copy-start.3
  6.5 34.0 %shard_map.127 = bf16[48,1152]{1,0:T(8,128)(2,1)S(1)} custom-call(bf16[48,1024]{1,0:T(8,128)(2,1)S(1)} %copy-done.2, f32[16,1024]{1,0:T(8,128)S(1)} %reshape.166.gain_ref, bf16[16384,1024]{1,0:T(8,128)(2,1)} %wq_hbm.1, bf16[64,16384]{1,0:T(8,128)(2,1)S(1)} %bitcast.32, bf16[64,16384]{1,0:T(8,128)(2,1)S(1)} %bitcast.33), custom_call_target="tpu_custom_call" | custom-call | tf_op jit(solution)/shard_map/pallas_call | solution.py:179
  40.5 0.2 convolution_convert_fusion
  40.7 0.7 reshape.167
  41.4 4.7 %all-to-all-start = ((bf16[16,4,1,1152]{3,1,2,0:T(4,128)(2,1)}), bf16[16,4,1,1152]{3,1,2,0:T(4,128)(2,1)S(1)}, u32[]{:S(2)}, u32[]{:S(2)}) async-start(bf16[16,4,1,1152]{3,1,2,0:T(4,128)(2,1)} %bitcast.5), calls=%async_computation | async-start | bytes 294912 | tf_op jit(solution)/shard_map/all_to_all | solution.py:358
  46.1 0.0 copy-done.7
  46.2 0.0 copy-done.5
  46.2 0.1 select_reduce_fusion.2
  46.3 0.0 copy-done.6
  46.3 0.1 select_reduce_fusion.1
  46.4 0.1 iota_add_fusion
  46.5 0.0 copy-done.4
  46.5 0.1 multiply_cosine_fusion
  46.6 0.1 add.58
  46.7 0.1 broadcast_in_dim.67
  46.8 0.1 eq.96
  46.8 0.7 copy.49.destination_ref
  47.5 0.1 broadcast_in_dim.63
  47.6 0.7 mul.150.key_factor_ref
  48.3 0.0 copy-done.3
  48.3 0.1 broadcast_in_dim.64
  48.4 0.7 reshape.170.value_factor_ref
  49.1 0.7 fusion.3.live_ref
  49.8 3.5 %all-to-all-done = bf16[16,4,1,1152]{3,1,2,0:T(4,128)(2,1)S(1)} async-done(((bf16[16,4,1,1152]{3,1,2,0:T(4,128)(2,1)}), bf16[16,4,1,1152]{3,1,2,0:T(4,128)(2,1)S(1)}, u32[]{:S(2)}, u32[]{:S(2)}) %all-to-all-start) | async-done | bytes 147488 | tf_op jit(solution)/shard_map/all_to_all | solution.py:358
  53.3 0.1 slice_convert_fusion.1
  53.4 0.1 reshape.172
  53.5 0.1 subtract_convert_fusion.1
  53.6 0.1 convert_bitcast_fusion
  53.6 0.6 copy.54
  54.3 0.1 subtract_convert_fusion
  54.5 0.1 maximum_bitcast_fusion
  54.6 0.7 copy.48
  55.2 0.7 reshape.174.value_ref
  55.9 37.5 %shard_map.128 = bf16[48,1024]{1,0:T(8,128)(2,1)} custom-call(bf16[16384,1024]{1,0:T(8,128)(2,1)} %wo_hbm.1, bf16[1024,1024]{1,0:T(8,128)(2,1)} %bitcast.34, bf16[1024,1024]{1,0:T(8,128)(2,1)} %bitcast.35, bf16[8,64,128]{2,1,0:T(8,128)(2,1)} %bitcast.38, f32[4,1024]{1,0:T(4,128)} %bitcast.41, f32[4,1024]{1,0:T(4,128)} %reshape.174.value_ref, ...), custom_call_target="tpu_custom_call" | custom-call | tf_op jit(solution)/shard_map/pallas_call | solution.py:306
  93.4 1.5 %copy.56 = bf16[48,1024]{1,0:T(8,128)(2,1)} copy(bf16[48,1024]{1,0:T(8,128)(2,1)} %shard_map.128) | data formatting | bytes 196608
  (9 shorter events, 0.1 us)
Async XLA Ops:
  2.4 1.6 %copy-start = (bf16[16384,64]{0,1:T(8,128)(2,1)S(1)}, bf16[16384,64]{0,1:T(8,128)(2,1)}, u32[]{:S(2)}) copy-start(bf16[16384,64]{0,1:T(8,128)(2,1)} %param.16) | copy-start | bytes 6291460
  4.0 1.6 %copy-start.1 = (bf16[16384,64]{0,1:T(8,128)(2,1)S(1)}, bf16[16384,64]{0,1:T(8,128)(2,1)}, u32[]{:S(2)}) copy-start(bf16[16384,64]{0,1:T(8,128)(2,1)} %param.17) | copy-start | bytes 6291460
  5.6 0.9 copy-start.2
  6.5 39.6 %copy-start.7 = (s32[48,1]{0,1:T(1,128)S(1)}, s32[48,1]{0,1:T(1,128)}, u32[]{:S(2)}) copy-start(s32[48,1]{0,1:T(1,128)} %param.23) | copy-start | bytes 580
  6.5 39.7 %copy-start.5 = (s32[48]{0:T(128)S(1)}, s32[48]{0:T(128)}, u32[]{:S(2)}) copy-start(s32[48]{0:T(128)} %param.24) | copy-start | bytes 580
  6.5 39.8 %copy-start.6 = (s32[1,16]{1,0:T(1,128)S(1)}, s32[1,16]{1,0:T(1,128)}, u32[]{:S(2)}) copy-start(s32[1,16]{1,0:T(1,128)} %param.25) | copy-start | bytes 196
  6.5 40.0 %copy-start.4 = (f32[16,8]{0,1:T(8,128)S(1)}, f32[16,8]{0,1:T(8,128)}, u32[]{:S(2)}) copy-start(f32[16,8]{0,1:T(8,128)} %param.21) | copy-start | bytes 1540
  6.5 41.8 %copy-start.3 = (f32[16,8]{0,1:T(8,128)S(1)}, f32[16,8]{0,1:T(8,128)}, u32[]{:S(2)}) copy-start(f32[16,8]{0,1:T(8,128)} %param.22) | copy-start | bytes 1540
  41.4 11.9 %all-to-all-start = ((bf16[16,4,1,1152]{3,1,2,0:T(4,128)(2,1)}), bf16[16,4,1,1152]{3,1,2,0:T(4,128)(2,1)S(1)}, u32[]{:S(2)}, u32[]{:S(2)}) async-start(bf16[16,4,1,1152]{3,1,2,0:T(4,128)(2,1)} %bitcast.5), calls=%async_computation | async-start | bytes 294912 | tf_op jit(solution)/shard_map/all_to_all | solution.py:358

commit v2 on v1

--- a/solution.py
+++ b/solution.py
@@ -58,58 +58,79 @@
     pl.semaphore_wait(barrier, len(peers))
 
 
-def gather(buffer, send_sems, recv_sems):
+def gather(buffer, send_sems, recv_sems, pieces):
     z, y, s, count = place()
-    line = line_order(z, count)
-    started = []
+    size = buffer.shape[1] // pieces
+    left = []
 
     def index(zz, yy, ss):
         return (zz * 2 + yy) * 2 + ss
 
-    def send(block, tensor, side):
-        copy = pltpu.make_async_remote_copy(
-            src_ref=buffer.at[block],
-            dst_ref=buffer.at[block],
-            send_sem=send_sems.at[len(started)],
-            recv_sem=recv_sems.at[block],
+    def when(have, action):
+        if have is None:
+            action()
+        else:
+            pl.when(have)(action)
+
+    def copy(block, piece, tensor, side, slot):
+        part = buffer.at[block, pl.ds(piece * size, size)]
+        return pltpu.make_async_remote_copy(
+            src_ref=part,
+            dst_ref=part,
+            send_sem=send_sems.at[slot],
+            recv_sem=recv_sems.at[block, piece],
             device_id={"tensor": tensor, "side": side},
             device_id_type=MESH,
         )
-        copy.start()
-        started.append(copy)
-
-    def arrived(block):
-        pltpu.make_async_remote_copy(
-            src_ref=buffer.at[block],
-            dst_ref=buffer.at[block],
-            send_sem=send_sems.at[0],
-            recv_sem=recv_sems.at[block],
-            device_id={"tensor": z * 2 + y, "side": 1 - s},
-            device_id_type=MESH,
-        ).wait_recv()
-
+
+    def send(have, block, piece, tensor, side):
+        slot = len(left)
+        when(have, lambda: copy(block, piece, tensor, side, slot).start())
+        left.append(
+            lambda: when(have, lambda: copy(block, piece, tensor, side, slot).wait_send())
+        )
+
+    def arrived(have, block, piece):
+        when(have, lambda: copy(block, piece, z * 2 + y, 1 - s, 0).wait_recv())
+
+    here, across = z * 2 + y, z * 2 + 1 - y
     me = index(z, y, s)
-    for zz in line[1:]:
-        send(me, zz * 2 + y, s)
-    send(me, z * 2 + 1 - y, s)
-    send(me, z * 2 + y, 1 - s)
+    for piece in range(pieces):
+        send(z < count - 1, me, piece, here + 2, s)
+        send(z > 0, me, piece, here - 2, s)
+        send(None, me, piece, across, s)
+        send(None, me, piece, here, 1 - s)
     for k in range(1, count + 1):
-        if k < count:
-            block = index(line[k], y, s)
-            arrived(block)
-            send(block, z * 2 + 1 - y, s)
-            send(block, z * 2 + y, 1 - s)
-        block = index(line[k - 1], 1 - y, s)
-        arrived(block)
-        send(block, z * 2 + y, 1 - s)
-    for zz in line:
+        for piece in range(pieces):
+            if k < count:
+                low, high = index(z - k, y, s), index(z + k, y, s)
+                arrived(z >= k, low, piece)
+                send((z >= k) & (z < count - 1), low, piece, here + 2, s)
+                send(z >= k, low, piece, across, s)
+                arrived(z + k < count, high, piece)
+                send((z + k < count) & (z > 0), high, piece, here - 2, s)
+                send(z + k < count, high, piece, across, s)
+                send(z >= k, low, piece, here, 1 - s)
+                send(z + k < count, high, piece, here, 1 - s)
+            if k == 1:
+                block = index(z, 1 - y, s)
+                arrived(None, block, piece)
+                send(None, block, piece, here, 1 - s)
+            else:
+                low, high = index(z - k + 1, 1 - y, s), index(z + k - 1, 1 - y, s)
+                arrived(z >= k - 1, low, piece)
+                send(z >= k - 1, low, piece, here, 1 - s)
+                arrived(z + k - 1 < count, high, piece)
+                send(z + k - 1 < count, high, piece, here, 1 - s)
+    for zz in line_order(z, count):
         for yy in (y, 1 - y):
-            arrived(index(zz, yy, 1 - s))
-    return started
+            for piece in range(pieces):
+                arrived(None, index(zz, yy, 1 - s), piece)
+    return left
 
 
 def project_kernel(
-    owners, x_ref, gain_ref, wq_hbm, key_hbm, value_hbm, out_ref,
+    owners, pieces, x_ref, gain_ref, wq_hbm, key_hbm, value_hbm, out_ref,
     buffer, wq_ref, kv_ref, total, total_kv, w_sems, kv_sems, send_sems, recv_sems,
 ):
     depth = x_ref.shape[1]
@@ -132,7 +153,7 @@
     z, y, s, _ = place()
     buffer[(z * 2 + y) * 2 + s] = x_ref[...]
     enter()
-    started = gather(buffer, send_sems, recv_sems)
+    started = gather(buffer, send_sems, recv_sems, pieces)
 
     def squares(c, acc):
         x = buffer[c].astype(jnp.float32)
@@ -167,17 +188,18 @@
 
     out_ref[:, :query_columns] = total[...].astype(jnp.bfloat16)
     out_ref[:, query_columns:] = total_kv[...].astype(jnp.bfloat16)
-    for copy in started:
-        copy.wait_send()
+    for wait in started:
+        wait()
 
 
 def project(owners, hidden_in, norm_gain, w_query, key_projection, value_projection):
     rows, depth = hidden_in.shape
     columns, kv_columns = w_query.shape[1], key_projection.shape[1]
-    sends = owners - 1
+    pieces = 3 if owners <= 16 else 1
+    sends = (2 * owners - 3) * pieces
     vmem, anywhere = pl.BlockSpec(memory_space=pltpu.VMEM), pl.BlockSpec(memory_space=pl.ANY)
     return pl.pallas_call(
-        functools.partial(project_kernel, owners),
+        functools.partial(project_kernel, owners, pieces),
         out_shape=jax.ShapeDtypeStruct((rows, columns + 2 * kv_columns), jnp.bfloat16),
         in_specs=[vmem, vmem, anywhere, anywhere, anywhere],
         out_specs=vmem,
@@ -190,16 +212,16 @@
             pltpu.SemaphoreType.DMA((owners,)),
             pltpu.SemaphoreType.DMA((2,)),
             pltpu.SemaphoreType.DMA((sends,)),
-            pltpu.SemaphoreType.DMA((owners,)),
+            pltpu.SemaphoreType.DMA((owners, pieces)),
         ],
         compiler_params=pltpu.CompilerParams(
-            collective_id=0, has_side_effects=True, vmem_limit_bytes=46 * 2**20
+            collective_id=0, has_side_effects=True, vmem_limit_bytes=58 * 2**20
         ),
     )(hidden_in, norm_gain.reshape(owners, depth), w_query, key_projection.T, value_projection.T)
 
 
 def attend_kernel(
-    owners, wo_hbm, keys_ref, values_ref, query_ref, key_ref, value_ref, key_factor_ref,
+    owners, pieces, wo_hbm, keys_ref, values_ref, query_ref, key_ref, value_ref, key_factor_ref,
     value_factor_ref, live_ref, destination_ref, out_ref,
     wo_ref, mixed, buffer, picked, total, w_sems, send_sems, recv_sems,
 ):
@@ -251,7 +273,7 @@
             pl.ds(j, block_rows, stride=GROUP_QUERIES), :
         ].astype(jnp.bfloat16)
     enter()
-    started = gather(buffer, send_sems, recv_sems)
+    started = gather(buffer, send_sems, recv_sems, pieces)
 
     per = min(owners, 16)
     step = KEY_VALUE_HEADS if owners <= 16 else 1
@@ -295,16 +317,17 @@
         total[...] += jnp.dot(picked[g], wo_ref[part, :], preferred_element_type=jnp.float32)
 
     out_ref[...] = total[...].astype(jnp.bfloat16)
-    for copy in started:
-        copy.wait_send()
+    for wait in started:
+        wait()
 
 
 def attend(owners, rows, w_out, *operands):
-    sends = owners - 1
+    pieces = 2 if owners <= 16 else 1
+    sends = (2 * owners - 3) * pieces
     block_rows = KEY_VALUE_HEADS * OWNER_ROW_SLOTS
     vmem, anywhere = pl.BlockSpec(memory_space=pltpu.VMEM), pl.BlockSpec(memory_space=pl.ANY)
     return pl.pallas_call(
-        functools.partial(attend_kernel, owners),
+        functools.partial(attend_kernel, owners, pieces),
         out_shape=jax.ShapeDtypeStruct((rows, w_out.shape[1]), jnp.bfloat16),
         in_specs=[anywhere] + [vmem] * len(operands),
         out_specs=vmem,
@@ -316,7 +339,7 @@
             pltpu.VMEM((rows, w_out.shape[1]), jnp.float32),
             pltpu.SemaphoreType.DMA((KEY_VALUE_HEADS,)),
             pltpu.SemaphoreType.DMA((sends,)),
-            pltpu.SemaphoreType.DMA((owners,)),
+            pltpu.SemaphoreType.DMA((owners, pieces)),
         ],
         compiler_params=pltpu.CompilerParams(
             collective_id=1, has_side_effects=True, vmem_limit_bytes=56 * 2**20

time: 95.4 us -> 89.7 us (0.940)
  local copies, waits for them, and re-layouts: 11.7 us -> 8.29 us
  Pallas kernels: 71.5 us -> 69.2 us
    unnamed x18 -> x12, local copies, waits for them, and re-layouts: 6.24 us -> 2.17 us
    pallas_call x2, Pallas kernels: 71.5 us -> 69.2 us  [the longest x1 35.5 us: project(): pl.pallas_call(functools.partial(project_kernel, owners, pieces), out_sha...]
where the time goes in v2:
time: 89.7 us; the launch traced here: 89.3 us
  Pallas kernels  69.2 us (77%)
  local copies, waits for them, and re-layouts  8.29 us (9%)
  starting transfers between devices  3.9 us (4%)
  waiting for transfers between devices  3.52 us (4%)
  other arithmetic  3.2 us (4%)
  matrix products  1.07 us (1%)
    pallas_call x1, Pallas kernels, project(): pl.pallas_call(functools.partial(project_kernel, owners, pieces), out_sha...  35.5 us
    pallas_call x1, Pallas kernels, attend(): pl.pallas_call(functools.partial(attend_kernel, owners, pieces), out_shap...  33.8 us
    all_to_all x1, starting transfers between devices, per_device(): lax.all_to_all(outgoing.reshape(owners, OWNER_ROW_SLOTS, 1, feature_count...  3.9 us
    all_to_all x1, waiting for transfers between devices, per_device(): lax.all_to_all(outgoing.reshape(owners, OWNER_ROW_SLOTS, 1, feature_count...  3.52 us
    unnamed x12, local copies, waits for them, and re-layouts  2.17 us
  transfers between devices with their start and end apart: 1, of which 1 were waited for; matrix products, arithmetic and copies ran while one was open for 4% of the time, Pallas kernels for 0%

profile of v2, /device:TPU:1, one launch (start us, length us, event | category | flops | bytes accessed | tf_op | source)
XLA Modules:
  0.0 89.3 jit_solution(14726053365675912500)
XLA Ops:
  0.0 0.9 %select_reduce_fusion = s32[48]{0:T(128)S(1)} fusion(s32[48]{0:T(128)} %bitcast.44), kind=kLoop, calls=%fused_computation.7 | loop fusion | flops 11472 | bytes 384 | tf_op jit(solution)/shard_map/reduce_sum | solution.py:374
  0.9 0.7 multiply_add_fusion
  1.6 1.5 %reshape.166.gain_ref = f32[16,1024]{1,0:T(8,128)} reshape(f32[16384]{0:T(1024)} %param.14) | data formatting | bytes 131072 | tf_op jit(solution)/shard_map/reshape | solution.py:220
  3.1 0.0 copy-start.4
  3.1 0.0 copy-start.2
  3.1 0.0 copy-start.3
  3.1 0.0 copy-start.1
  3.1 0.0 copy-start
  3.1 35.5 %shard_map.127 = bf16[48,1152]{1,0:T(8,128)(2,1)} custom-call(bf16[48,1024]{1,0:T(8,128)(2,1)} %x_ref.1, f32[16,1024]{1,0:T(8,128)} %reshape.166.gain_ref, bf16[16384,1024]{1,0:T(8,128)(2,1)} %wq_hbm.1, bf16[64,16384]{1,0:T(8,128)(2,1)} %bitcast.32, bf16[64,16384]{1,0:T(8,128)(2,1)} %bitcast.33), custom_call_target="tpu_custom_call" | custom-call | tf_op jit(solution)/shard_map/pallas_call | solution.py:201
  38.6 1.1 %convolution_convert_fusion = bf16[64,1152]{1,0:T(8,128)(2,1)S(1)} fusion(bf16[48,1152]{1,0:T(8,128)(2,1)} %shard_map.127, s32[48]{0:T(128)S(1)} %multiply_add_fusion), kind=kOutput, calls=%fused_computation | convolution fusion | flops 7154688 | bytes 258240 | tf_op jit(solution)/shard_map/dot_general | solution.py:380
  39.6 0.7 reshape.167
  40.3 3.9 %all-to-all-start = ((bf16[16,4,1,1152]{3,1,2,0:T(4,128)(2,1)}), bf16[16,4,1,1152]{3,1,2,0:T(4,128)(2,1)S(1)}, u32[]{:S(2)}, u32[]{:S(2)}) async-start(bf16[16,4,1,1152]{3,1,2,0:T(4,128)(2,1)} %bitcast.5), calls=%async_computation | async-start | bytes 294912 | tf_op jit(solution)/shard_map/all_to_all | solution.py:381
  44.2 0.0 copy-done.4
  44.3 0.0 copy-done.2
  44.3 0.1 select_reduce_fusion.2
  44.4 0.0 copy-done.3
  44.4 0.1 select_reduce_fusion.1
  44.5 0.1 iota_add_fusion
  44.6 0.0 copy-done.1
  44.6 0.1 multiply_cosine_fusion
  44.7 0.1 add.58
  44.8 0.1 broadcast_in_dim.67
  44.9 0.1 eq.96
  44.9 0.7 copy.49.destination_ref
  45.6 0.1 broadcast_in_dim.63
  45.7 0.7 mul.150.key_factor_ref
  46.4 0.0 copy-done
  46.4 0.1 broadcast_in_dim.64
  46.5 0.7 reshape.170.value_factor_ref
  47.2 0.7 fusion.3.live_ref
  47.9 3.5 %all-to-all-done = bf16[16,4,1,1152]{3,1,2,0:T(4,128)(2,1)S(1)} async-done(((bf16[16,4,1,1152]{3,1,2,0:T(4,128)(2,1)}), bf16[16,4,1,1152]{3,1,2,0:T(4,128)(2,1)S(1)}, u32[]{:S(2)}, u32[]{:S(2)}) %all-to-all-start) | async-done | bytes 147488 | tf_op jit(solution)/shard_map/all_to_all | solution.py:381
  51.4 0.1 slice_convert_fusion.1
  51.5 0.1 reshape.172
  51.6 0.1 subtract_convert_fusion.1
  51.7 0.1 convert_bitcast_fusion
  51.7 0.6 copy.54
  52.4 0.1 subtract_convert_fusion
  52.5 0.1 maximum_bitcast_fusion
  52.7 0.7 copy.48
  53.3 0.7 reshape.174.value_ref
  54.0 33.8 %shard_map.128 = bf16[48,1024]{1,0:T(8,128)(2,1)} custom-call(bf16[16384,1024]{1,0:T(8,128)(2,1)} %wo_hbm.1, bf16[1024,1024]{1,0:T(8,128)(2,1)} %bitcast.34, bf16[1024,1024]{1,0:T(8,128)(2,1)} %bitcast.35, bf16[8,64,128]{2,1,0:T(8,128)(2,1)} %bitcast.38, f32[4,1024]{1,0:T(4,128)} %bitcast.41, f32[4,1024]{1,0:T(4,128)} %reshape.174.value_ref, ...), custom_call_target="tpu_custom_call" | custom-call | tf_op jit(solution)/shard_map/pallas_call | solution.py:329
  87.8 1.5 %copy.56 = bf16[48,1024]{1,0:T(8,128)(2,1)} copy(bf16[48,1024]{1,0:T(8,128)(2,1)} %shard_map.128) | data formatting | bytes 196608
  (9 shorter events, 0.1 us)
Async XLA Ops:
  3.1 41.2 %copy-start.4 = (s32[48,1]{0,1:T(1,128)S(1)}, s32[48,1]{0,1:T(1,128)}, u32[]{:S(2)}) copy-start(s32[48,1]{0,1:T(1,128)} %param.23) | copy-start | bytes 580
  3.1 41.2 %copy-start.2 = (s32[48]{0:T(128)S(1)}, s32[48]{0:T(128)}, u32[]{:S(2)}) copy-start(s32[48]{0:T(128)} %param.24) | copy-start | bytes 580
  3.1 41.3 %copy-start.3 = (s32[1,16]{1,0:T(1,128)S(1)}, s32[1,16]{1,0:T(1,128)}, u32[]{:S(2)}) copy-start(s32[1,16]{1,0:T(1,128)} %param.25) | copy-start | bytes 196
  3.1 41.5 %copy-start.1 = (f32[16,8]{0,1:T(8,128)S(1)}, f32[16,8]{0,1:T(8,128)}, u32[]{:S(2)}) copy-start(f32[16,8]{0,1:T(8,128)} %param.21) | copy-start | bytes 1540
  3.1 43.3 %copy-start = (f32[16,8]{0,1:T(8,128)S(1)}, f32[16,8]{0,1:T(8,128)}, u32[]{:S(2)}) copy-start(f32[16,8]{0,1:T(8,128)} %param.22) | copy-start | bytes 1540
  40.3 11.1 %all-to-all-start = ((bf16[16,4,1,1152]{3,1,2,0:T(4,128)(2,1)}), bf16[16,4,1,1152]{3,1,2,0:T(4,128)(2,1)S(1)}, u32[]{:S(2)}, u32[]{:S(2)}) async-start(bf16[16,4,1,1152]{3,1,2,0:T(4,128)(2,1)} %bitcast.5), calls=%async_computation | async-start | bytes 294912 | tf_op jit(solution)/shard_map/all_to_all | solution.py:381

commit v3 on v2

--- a/solution.py
+++ b/solution.py
@@ -56,6 +56,24 @@
             barrier, inc=1, device_id={"tensor": tensor, "side": side}, device_id_type=MESH
         )
     pl.semaphore_wait(barrier, len(peers))
+
+
+def enter_all(owners):
+    z, y, s, _ = place()
+    me = (z * 2 + y) * 2 + s
+    barrier = pltpu.get_barrier_semaphore()
+
+    @pl.loop(1, owners)
+    def _(k):
+        other = lax.rem(me + k, owners)
+        pl.semaphore_signal(
+            barrier,
+            inc=1,
+            device_id={"tensor": other // 2, "side": lax.rem(other, 2)},
+            device_id_type=MESH,
+        )
+
+    pl.semaphore_wait(barrier, owners - 1)
 
 
 def gather(buffer, send_sems, recv_sems, pieces):
@@ -130,8 +148,9 @@
 
 
 def project_kernel(
-    owners, pieces, x_ref, gain_ref, wq_hbm, key_hbm, value_hbm, out_ref,
-    buffer, wq_ref, kv_ref, total, total_kv, w_sems, kv_sems, send_sems, recv_sems,
+    owners, pieces, x_ref, gain_ref, code_ref, wq_hbm, key_hbm, value_hbm, out_ref,
+    buffer, wq_ref, kv_ref, total, total_kv, outbox, inbox,
+    w_sems, kv_sems, send_sems, recv_sems, out_sems, in_sems,
 ):
     depth = x_ref.shape[1]
     kv_columns = key_hbm.shape[0]
@@ -151,8 +170,9 @@
         weights(c).start()
 
     z, y, s, _ = place()
-    buffer[(z * 2 + y) * 2 + s] = x_ref[...]
-    enter()
+    me = (z * 2 + y) * 2 + s
+    buffer[me] = x_ref[...]
+    enter_all(owners)
     started = gather(buffer, send_sems, recv_sems, pieces)
 
     def squares(c, acc):
@@ -186,22 +206,93 @@
         weights(c).wait()
         total[...] += jnp.dot(normed, wq_ref[columns, :], preferred_element_type=jnp.float32)
 
-    out_ref[:, :query_columns] = total[...].astype(jnp.bfloat16)
-    out_ref[:, query_columns:] = total_kv[...].astype(jnp.bfloat16)
+    heads = query_columns // HEAD_SIZE
+    slots = owners * OWNER_ROW_SLOTS
+    shape = (owners, outbox.shape[1], code_ref.shape[1])
+    inner = lax.broadcasted_iota(jnp.int32, shape, 1)
+    wanted = (
+        jnp.minimum(inner >> 2, heads) * slots
+        + lax.broadcasted_iota(jnp.int32, shape, 0) * OWNER_ROW_SLOTS
+        + (inner & 3)
+    ).reshape(shape[0] * shape[1], shape[2])
+    pick = jnp.where(wanted == code_ref[...], 1.0, 0.0).astype(jnp.bfloat16)
+    both = total_kv[...].astype(jnp.bfloat16)
+    if 2 * kv_columns < HEAD_SIZE:
+        spare = jnp.zeros((both.shape[0], HEAD_SIZE - 2 * kv_columns), jnp.bfloat16)
+        both = jnp.concatenate([both, spare], axis=1)
+    stacked = [
+        total[:, h * HEAD_SIZE : (h + 1) * HEAD_SIZE].astype(jnp.bfloat16) for h in range(heads)
+    ]
+    outbox[...] = (
+        jnp.dot(
+            pick,
+            jnp.concatenate(stacked + [both], axis=0),
+            preferred_element_type=jnp.float32,
+        )
+        .astype(jnp.bfloat16)
+        .reshape(outbox.shape)
+    )
+
+    def delivery(k):
+        other = lax.rem(me + k, owners)
+        return pltpu.make_async_remote_copy(
+            src_ref=outbox.at[other],
+            dst_ref=inbox.at[me],
+            send_sem=out_sems.at[other],
+            recv_sem=in_sems.at[me],
+            device_id={"tensor": other // 2, "side": lax.rem(other, 2)},
+            device_id_type=MESH,
+        )
+
+    def receipt(k):
+        other = lax.rem(me + k, owners)
+        return pltpu.make_async_remote_copy(
+            src_ref=outbox.at[other],
+            dst_ref=inbox.at[other],
+            send_sem=out_sems.at[other],
+            recv_sem=in_sems.at[other],
+            device_id={"tensor": other // 2, "side": lax.rem(other, 2)},
+            device_id_type=MESH,
+        )
+
+    @pl.loop(1, owners)
+    def _(k):
+        delivery(k).start()
+
+    inbox[me] = outbox[me]
+
+    @pl.loop(1, owners)
+    def _(k):
+        receipt(k).wait_recv()
+
+    out_ref[...] = inbox[...]
+
+    @pl.loop(1, owners)
+    def _(k):
+        delivery(k).wait_send()
+
     for wait in started:
         wait()
 
 
-def project(owners, hidden_in, norm_gain, w_query, key_projection, value_projection):
+def project(
+    owners, destination, hidden_in, norm_gain, w_query, key_projection, value_projection
+):
     rows, depth = hidden_in.shape
     columns, kv_columns = w_query.shape[1], key_projection.shape[1]
+    heads = columns // HEAD_SIZE
+    box = (owners, -(-(heads + 1) * OWNER_ROW_SLOTS // 16) * 16, HEAD_SIZE)
+    code = (
+        jnp.arange(heads + 1, dtype=jnp.int32)[:, None] * (owners * OWNER_ROW_SLOTS)
+        + destination[None, :].astype(jnp.int32)
+    ).reshape(1, (heads + 1) * rows)
     pieces = 3 if owners <= 16 else 1
     sends = (2 * owners - 3) * pieces
     vmem, anywhere = pl.BlockSpec(memory_space=pltpu.VMEM), pl.BlockSpec(memory_space=pl.ANY)
     return pl.pallas_call(
         functools.partial(project_kernel, owners, pieces),
-        out_shape=jax.ShapeDtypeStruct((rows, columns + 2 * kv_columns), jnp.bfloat16),
-        in_specs=[vmem, vmem, anywhere, anywhere, anywhere],
+        out_shape=jax.ShapeDtypeStruct(box, jnp.bfloat16),
+        in_specs=[vmem, vmem, vmem, anywhere, anywhere, anywhere],
         out_specs=vmem,
         scratch_shapes=[
             pltpu.VMEM((owners, rows, depth), jnp.bfloat16),
@@ -209,15 +300,26 @@
             pltpu.VMEM((2, kv_columns, owners * depth), jnp.bfloat16),
             pltpu.VMEM((rows, columns), jnp.float32),
             pltpu.VMEM((rows, 2 * kv_columns), jnp.float32),
+            pltpu.VMEM(box, jnp.bfloat16),
+            pltpu.VMEM(box, jnp.bfloat16),
             pltpu.SemaphoreType.DMA((owners,)),
             pltpu.SemaphoreType.DMA((2,)),
             pltpu.SemaphoreType.DMA((sends,)),
             pltpu.SemaphoreType.DMA((owners, pieces)),
+            pltpu.SemaphoreType.DMA((owners,)),
+            pltpu.SemaphoreType.DMA((owners,)),
         ],
         compiler_params=pltpu.CompilerParams(
             collective_id=0, has_side_effects=True, vmem_limit_bytes=58 * 2**20
         ),
-    )(hidden_in, norm_gain.reshape(owners, depth), w_query, key_projection.T, value_projection.T)
+    )(
+        hidden_in,
+        norm_gain.reshape(owners, depth),
+        code,
+        w_query,
+        key_projection.T,
+        value_projection.T,
+    )
 
 
 def attend_kernel(
@@ -366,35 +468,29 @@
     my_index = lax.axis_index(("tensor", "side"))
     row_count = hidden_in.shape[0]
     query_group_count = QUERY_HEADS // KEY_VALUE_HEADS
-    packed = project(owners, hidden_in, norm_gain, w_query, key_projection, value_projection)
     owner_ids = row_owner[:, 0]
     row_numbers = jnp.arange(row_count)
     same_owner = owner_ids[:, None] == owner_ids[None, :]
     earlier = row_numbers[None, :] < row_numbers[:, None]
     slot_index = jnp.sum(jnp.where(same_owner & earlier, 1, 0), axis=1).astype(jnp.int32)
     destination = owner_ids * OWNER_ROW_SLOTS + slot_index
-    feature_count = packed.shape[1]
-    one_hot = (jnp.arange(owners * OWNER_ROW_SLOTS)[:, None] == destination[None, :]).astype(
-        jnp.bfloat16
-    )
-    outgoing = jnp.dot(one_hot, packed, preferred_element_type=jnp.float32).astype(jnp.bfloat16)
-    received_part = lax.all_to_all(
-        outgoing.reshape(owners, OWNER_ROW_SLOTS, 1, feature_count),
-        ("tensor", "side"),
-        split_axis=0,
-        concat_axis=2,
-        tiled=True,
-    )
-    received_part = received_part.reshape(OWNER_ROW_SLOTS, owners, feature_count)
-    query_columns = w_query.shape[1]
+    received = project(
+        owners, destination, hidden_in, norm_gain, w_query, key_projection, value_projection
+    )
+    heads = w_query.shape[1] // HEAD_SIZE
     key_columns = key_projection.shape[1]
-    query_all = received_part[:, :, :query_columns].reshape(
-        OWNER_ROW_SLOTS, QUERY_HEADS * HEAD_SIZE
-    )
-    every_key = received_part[:, :, query_columns : query_columns + key_columns].reshape(
+    query_all = jnp.swapaxes(
+        received[:, : heads * OWNER_ROW_SLOTS].reshape(QUERY_HEADS, OWNER_ROW_SLOTS, HEAD_SIZE),
+        0,
+        1,
+    )
+    pair = jnp.swapaxes(
+        received[:, heads * OWNER_ROW_SLOTS : (heads + 1) * OWNER_ROW_SLOTS], 0, 1
+    )
+    every_key = pair[:, :, :key_columns].reshape(
         OWNER_ROW_SLOTS, KEY_VALUE_HEADS * HEAD_SIZE
     )
-    every_value = received_part[:, :, query_columns + key_columns :].reshape(
+    every_value = pair[:, :, key_columns : 2 * key_columns].reshape(
         OWNER_ROW_SLOTS, KEY_VALUE_HEADS * HEAD_SIZE
     )
     mine = owner_ids == my_index

time: 89.7 us -> 92 us (1.026)
  Pallas kernels: 69.2 us -> 77 us
  starting transfers between devices: 3.9 us -> 0 us
  waiting for transfers between devices: 3.52 us -> 0 us
  other arithmetic: 3.2 us -> 5.49 us
  matrix products: 1.07 us -> 0 us
    pallas_call x1, Pallas kernels: 35.5 us -> 40.8 us  [project(): pl.pallas_call(functools.partial(project_kernel, owners, pieces), out_sha...]
    all_to_all x1 -> x0, starting transfers between devices: 3.9 us -> none  [per_device(): lax.all_to_all(outgoing.reshape(owners, OWNER_ROW_SLOTS, 1, feature_count...]
    all_to_all x1 -> x0, waiting for transfers between devices: 3.52 us -> none  [per_device(): lax.all_to_all(outgoing.reshape(owners, OWNER_ROW_SLOTS, 1, feature_count...]
    pallas_call x1, Pallas kernels: 33.8 us -> 36.2 us  [attend(): pl.pallas_call(functools.partial(attend_kernel, owners, pieces), out_shap...]
    dot_general x1 -> x0, matrix products: 1.07 us -> none  [per_device(): jnp.dot(one_hot, packed, preferred_element_type=jnp.float32)]
    unnamed x12 -> x10, local copies, waits for them, and re-layouts: 2.17 us -> 2.18 us
  transfers between devices with their start and end apart: 1 -> 0, of which waited for: 1 -> 0; matrix products, arithmetic and copies ran while one was open for 4% -> 0% of each run, Pallas kernels for 0% -> 0%
where the time goes in v3:
time: 92 us; the launch traced here: 91.6 us
  Pallas kernels  77 us (84%)
  local copies, waits for them, and re-layouts  9.01 us (10%)
  other arithmetic  5.49 us (6%)
    pallas_call x1, Pallas kernels, project(): pl.pallas_call(functools.partial(project_kernel, owners, pieces), out_sha...  40.8 us
    pallas_call x1, Pallas kernels, attend(): pl.pallas_call(functools.partial(attend_kernel, owners, pieces), out_shap...  36.2 us
    unnamed x10, local copies, waits for them, and re-layouts  2.18 us

profile of v3, /device:TPU:1, one launch (start us, length us, event | category | flops | bytes accessed | tf_op | source)
XLA Modules:
  0.0 91.6 jit_solution(4993994380216333852)
XLA Ops:
  0.0 0.7 broadcast_compare_fusion
  0.7 0.9 select_reduce_fusion
  1.6 0.8 select_reduce_fusion.2
  2.4 0.1 multiply_cosine_fusion
  2.5 0.7 multiply_add_fusion
  3.2 0.1 broadcast_add_fusion
  3.2 0.6 add.77.code_ref
  3.9 1.5 %reshape.185.gain_ref = f32[16,1024]{1,0:T(8,128)} reshape(f32[16384]{0:T(1024)} %param.14) | data formatting | bytes 131072 | tf_op jit(solution)/shard_map/reshape | solution.py:317
  5.4 40.8 %shard_map.127 = bf16[16,48,128]{2,1,0:T(8,128)(2,1)} custom-call(bf16[48,1024]{1,0:T(8,128)(2,1)} %x_ref.1, f32[16,1024]{1,0:T(8,128)} %reshape.185.gain_ref, s32[1,432]{1,0:T(1,128)} %add.77.code_ref, bf16[16384,1024]{1,0:T(8,128)(2,1)} %wq_hbm.1, bf16[64,16384]{1,0:T(8,128)(2,1)} %bitcast.32, bf16[64,16384]{1,0:T(8,128)(2,1)} %bitcast.33), custom_call_target="tpu_custom_call" | custom-call | tf_op jit(solution)/shard_map/pallas_call | solution.py:292
  46.1 0.0 copy-start.2
  46.2 0.0 copy-start.3
  46.2 0.0 copy-start.1
  46.2 0.0 copy-start
  46.2 0.8 slice_bitcast_fusion
  47.0 0.1 slice_convert_fusion.1
  47.1 0.1 reshape.188
  47.1 0.1 subtract_convert_fusion.1
  47.2 0.1 convert_bitcast_fusion
  47.3 0.6 copy.41
  47.9 0.9 %slice_convert_fusion = f32[16,32,128]{2,1,0:T(8,128)S(1)} fusion(bf16[16,48,128]{2,1,0:T(8,128)(2,1)} %shard_map.127), kind=kLoop, calls=%fused_computation.4 | loop fusion | flops 65536 | bytes 393216 | tf_op jit(solution)/shard_map/convert_element_type | solution.py:515
  48.9 0.1 subtract_convert_fusion
  49.0 0.1 maximum_bitcast_fusion
  49.1 0.7 copy.33
  49.8 0.0 copy-done.2
  49.8 0.1 select_reduce_fusion.1
  49.9 0.1 iota_add_fusion
  50.0 0.1 add.85
  50.0 0.1 broadcast_in_dim.67
  50.1 0.1 eq.80
  50.2 0.7 fusion.2.live_ref
  50.9 0.7 reshape.190.value_ref
  51.5 0.0 copy-done.3
  51.6 0.7 copy.36.destination_ref
  52.3 0.0 copy-done.1
  52.3 0.1 broadcast_in_dim.63
  52.3 0.7 mul.159.key_factor_ref
  53.0 0.0 copy-done
  53.0 0.1 broadcast_in_dim.64
  53.1 0.7 reshape.187.value_factor_ref
  53.8 36.2 %shard_map.128 = bf16[48,1024]{1,0:T(8,128)(2,1)} custom-call(bf16[16384,1024]{1,0:T(8,128)(2,1)} %wo_hbm.1, bf16[1024,1024]{1,0:T(8,128)(2,1)} %bitcast.34, bf16[1024,1024]{1,0:T(8,128)(2,1)} %bitcast.35, bf16[8,64,128]{2,1,0:T(8,128)(2,1)} %bitcast.37, f32[4,1024]{1,0:T(4,128)} %bitcast.40, f32[4,1024]{1,0:T(4,128)} %reshape.190.value_ref, ...), custom_call_target="tpu_custom_call" | custom-call | tf_op jit(solution)/shard_map/pallas_call | solution.py:431
  90.1 1.5 %copy.43 = bf16[48,1024]{1,0:T(8,128)(2,1)} copy(bf16[48,1024]{1,0:T(8,128)(2,1)} %shard_map.128) | data formatting | bytes 196608
  (9 shorter events, 0.1 us)
Async XLA Ops:
  46.1 3.7 %copy-start.2 = (s32[1,16]{1,0:T(1,128)S(1)}, s32[1,16]{1,0:T(1,128)}, u32[]{:S(2)}) copy-start(s32[1,16]{1,0:T(1,128)} %param.25) | copy-start | bytes 196
  46.2 5.4 %copy-start.3 = (s32[48,1]{0,1:T(1,128)S(1)}, s32[48,1]{0,1:T(1,128)}, u32[]{:S(2)}) copy-start(s32[48,1]{0,1:T(1,128)} %param.23) | copy-start | bytes 580
  46.2 6.1 %copy-start.1 = (f32[16,8]{0,1:T(8,128)S(1)}, f32[16,8]{0,1:T(8,128)}, u32[]{:S(2)}) copy-start(f32[16,8]{0,1:T(8,128)} %param.21) | copy-start | bytes 1540
  46.2 6.9 %copy-start = (f32[16,8]{0,1:T(8,128)S(1)}, f32[16,8]{0,1:T(8,128)}, u32[]{:S(2)}) copy-start(f32[16,8]{0,1:T(8,128)} %param.22) | copy-start | bytes 1540
